TPU v7x, 512 devices: a whole 4x4x16 slice. The times are simulated.
512 devices in a mesh: space: 128 (over z, x, core), basis: 4 (over y).
Axes of the slice: x: 4, y: 4, z: 16, core: 2. Of those that a mesh axis runs over, the one named last changes fastest.
Arguments:
- x_block: float32 [16, 3, 128, 32, 128], P(None, None, 'space', 'basis'), may hold values from -68 to 68
- basis: float32 [64, 3, 128, 32, 128], P('basis', None, 'space'), may hold values from -11 to 11
- material: int32 [128, 32, 128], P('space', 'basis'), may hold values from 0 to 7
- k0_blocks: float32 [8, 7, 3, 3], replicated, may hold values from -4 to 4
- k0_diag: float32 [8, 3], replicated, may hold values from 2 to 8
- ke_blocks: float32 [8, 7, 3, 3], replicated, may hold values from -6 to 6
- mass: float32 [8, 3], replicated, may hold values from 0.5 to 2
- velocities: float32 [1024], replicated, may hold values from 0.5 to 1
- shifts: float32 [1024], replicated, may hold values from 0.5 to 1.5
- sample: int32 [1], replicated, may hold values from 0 to 1023
Outputs:
- orthonormal: float32 [16, 3, 128, 32, 128], P(None, None, 'space', 'basis')
- coefficients: float32 [64, 16], P('basis')
- upper_factor: float32 [16, 16], replicated
All inputs are finite; a program needn't handle non-finite values.
Results may differ from a plain program's by a relative error of at most 0.00015.
Values sent between devices are 32-bit elements; how exact they have to be, the bound alone decides.
A program may use at most 64 MiB of HBM per device.

v0:
```python
import jax
import jax.numpy as jnp
from jax import lax
from jax.sharding import PartitionSpec as P

exact_precision = lax.Precision.HIGHEST


def with_halo(cells, sides, width):
    for axis, dim in sides:
        count = lax.axis_size(axis)
        ends = count - 1
        head = lax.slice_in_dim(cells, 0, width, axis=dim)
        tail = lax.slice_in_dim(cells, cells.shape[dim] - width, cells.shape[dim], axis=dim)
        cells = jnp.concatenate(
            [
                lax.ppermute(tail, axis, [(i, (i + 1) % count) for i in range(ends)]),
                cells,
                lax.ppermute(head, axis, [((i + 1) % count, i) for i in range(ends)]),
            ],
            axis=dim,
        )
    return cells


def stencil_tables(k0_blocks, k0_diag, ke_blocks, mass, velocities, shifts, sample):
    velocity = jnp.take(velocities, sample, axis=0)[0]
    sigma_value = jnp.take(shifts, sample, axis=0)[0]
    center = (k0_diag - sigma_value * mass)[:, :, None] * jnp.eye(3, dtype=jnp.float32)
    tables = k0_blocks - velocity * velocity * ke_blocks
    return tables.at[:, 0].add(center)


def neighbour_views(rimmed):
    centre = rimmed[:, :, 1:-1, 1:-1, :]
    lower_x = rimmed[:, :, :-2, 1:-1, :]
    upper_x = rimmed[:, :, 2:, 1:-1, :]
    lower_y = rimmed[:, :, 1:-1, :-2, :]
    upper_y = rimmed[:, :, 1:-1, 2:, :]
    zero_col = jnp.zeros(centre.shape[:4] + (1,), centre.dtype)
    lower_z = jnp.concatenate((zero_col, centre[:, :, :, :, :-1]), axis=4)
    upper_z = jnp.concatenate((centre[:, :, :, :, 1:], zero_col), axis=4)
    return [centre, lower_x, upper_x, lower_y, upper_y, lower_z, upper_z]


def cell_fields(tables, material_cells):
    material_count = tables.shape[0]
    fields = jnp.zeros((7, 3, 3) + material_cells.shape, jnp.float32)
    for level in range(material_count):
        chosen = (material_cells == level).astype(jnp.float32)
        fields = fields + tables[level][:, :, :, None, None, None] * chosen[None, None, None]
    return fields


def apply_fields(rimmed, fields):
    stencil_views = neighbour_views(rimmed)
    sums = [None, None, None]
    for offset in range(7):
        view = stencil_views[offset]
        for row in range(3):
            term = fields[offset, row, 0][None] * view[:, 0]
            term = term + fields[offset, row, 1][None] * view[:, 1]
            term = term + fields[offset, row, 2][None] * view[:, 2]
            sums[row] = term if sums[row] is None else sums[row] + term
    return jnp.stack(sums, axis=1)


def fine_image(x_block, material, tables):
    rimmed = with_halo(x_block, (("space", 2), ("basis", 3)), 1)
    return apply_fields(rimmed, cell_fields(tables, material))


def group_sum(partial_value):
    return lax.psum(partial_value, "space")


def scaled_block(fine_block, gram_matrix):
    block_cols = fine_block.shape[0]
    lower_factor = jnp.linalg.cholesky(gram_matrix)
    inverse = jax.scipy.linalg.solve_triangular(
        lower_factor, jnp.eye(block_cols, dtype=jnp.float32), lower=True
    ).T
    orthonormal = jnp.einsum("mcxyz,mn->ncxyz", fine_block, inverse, precision=exact_precision)
    return (orthonormal, lower_factor.T)


def finish(fine_block, row_count):
    gram_partial = jnp.einsum("ncxyz,mcxyz->nm", fine_block, fine_block, precision=exact_precision)
    gram_matrix = lax.psum(gram_partial, ("space", "basis")) / row_count
    return scaled_block(fine_block, gram_matrix)


def shards(
    x_block, basis, material, k0_blocks, k0_diag, ke_blocks, mass, velocities, shifts, sample
):
    tables = stencil_tables(k0_blocks, k0_diag, ke_blocks, mass, velocities, shifts, sample)
    block_cols = x_block.shape[0]
    extent_x = x_block.shape[2]
    extent_z = x_block.shape[4]
    full_y = basis.shape[3]
    group_cols = basis.shape[0]
    row_count = 3.0 * extent_x * lax.axis_size("space") * full_y * extent_z
    running = jnp.zeros((group_cols, block_cols), jnp.float32)
    fine_block = fine_image(x_block, material, tables)
    for repeat in range(2):
        partial_value = jnp.einsum(
            "kcxyz,ncxyz->kn",
            basis,
            lax.all_gather(fine_block, "basis", axis=3, tiled=True),
            precision=exact_precision,
        )
        local_coeffs = group_sum(partial_value) / row_count
        correction = jnp.einsum("kcxyz,kn->ncxyz", basis, local_coeffs, precision=exact_precision)
        fine_block = fine_block - lax.psum_scatter(
            correction, "basis", scatter_dimension=3, tiled=True
        )
        running = running + local_coeffs
    orthonormal, upper_factor = finish(fine_block, row_count)
    return (orthonormal, running, upper_factor)


def solution(mesh):
    in_specs = (
        P(None, None, "space", "basis", None),
        P("basis", None, "space", None, None),
        P("space", "basis", None),
        P(),
        P(),
        P(),
        P(),
        P(),
        P(),
        P(),
    )
    out_specs = (P(None, None, "space", "basis", None), P("basis", None), P())
    return jax.shard_map(shards, mesh=mesh, in_specs=in_specs, out_specs=out_specs, check_vma=False)
```

profile of v0, /device:TPU:1, one launch (start us, length us, event | category | flops | bytes accessed | tf_op | source)
XLA Modules:
  0.0 749.9 jit_solution(10074327521690366731)
XLA Ops:
  7.3 1.0 copy.71
  8.3 8.8 %collective-permute-start.1 = (f32[16,3,1,8,128]{4,0,3,1,2:T(8,128)S(1)}, f32[16,3,1,8,128]{4,0,3,1,2:T(8,128)S(1)}, u32[]{:S(2)}, u32[]{:S(2)}) collective-permute-start(f32[16,3,1,8,128]{4,0,3,1,2:T(8,128)S(1)} %copy.71), channel_id=1, source_target_pairs={{4,0},{8,4},{12,8},{16,12},{20,16},{24,20},{28,24},{32,28},{36,32}... | collective-permute-start | bytes 589832 | tf_op jit(solution)/shard_map/ppermute | solution.py:19
  17.1 1.9 collective-permute-start
  19.7 1.3 dynamic-slice.13
  21.0 1.3 dynamic-slice.12
  23.7 0.1 scatter-add.4
  23.9 0.1 copy.94
  24.0 0.1 copy.101
  24.1 0.1 copy.100
  24.2 0.1 copy.99
  24.3 0.1 copy.98
  24.4 0.1 copy.97
  24.5 0.1 copy.96
  24.6 0.1 copy.95
  24.7 0.6 multiply_add_fusion
  25.4 0.1 fusion.22
  25.6 0.9 copy-done.1
  26.6 1.3 collective-permute-start.3
  27.9 4.0 collective-permute-start.2
  31.9 1.4 collective-permute-done.2
  33.2 0.2 add_add_fusion.2
  33.4 0.2 add_add_fusion.1
  33.7 0.2 add_add_fusion
  33.9 11.9 %all_gather.6 = f32[16,3,1,32,128]{4,0,3,1,2:T(8,128)S(1)} all-gather(f32[16,3,1,8,128]{4,0,3,1,2:T(8,128)S(1)} %pad_maximum_fusion), channel_id=1, replica_groups=mesh['space'=128,'basis'=4] {'basis'}, dimensions={3}, use_global_device_ids=true | all-gather | bytes 983040 | tf_op jit(solution)/shard_map/all_gather | solution.py:109
  45.8 1.4 convolution_bitcast_fusion.4
  47.2 256.7 %psum.21 = f32[16,16]{0,1:T(8,128)S(1)} all-reduce(f32[16,16]{0,1:T(8,128)S(1)} %convolution_bitcast_fusion.4), channel_id=1, replica_groups=mesh['space'=128,'basis'=4] {'space'}, use_global_device_ids=true, to_apply=%region_0.1 | all-reduce | flops 256 | bytes 2048 | tf_op jit(solution)/shard_map/psum | solution.py:74
  303.9 1.1 convolution_bitcast_fusion.1
  305.1 1.1 copy.129
  306.3 26.9 %reduce-scatter.9.cloned.1.call-done = f32[8,6144]{1,0:T(8,128)} async-done(((f32[32,6144]{1,0:T(8,128)}), f32[8,6144]{1,0:T(8,128)}) %reduce-scatter.9.cloned.1.call-update) | async-done | bytes 196624
  333.2 1.0 copy.108
  334.2 11.1 %all_gather.7 = f32[16,3,1,32,128]{4,0,3,1,2:T(8,128)S(1)} all-gather(f32[16,3,1,8,128]{4,0,3,1,2:T(8,128)S(1)} %copy_subtract_fusion.1), channel_id=1, replica_groups=mesh['space'=128,'basis'=4] {'basis'}, dimensions={3}, use_global_device_ids=true | all-gather | bytes 983040 | tf_op jit(solution)/shard_map/all_gather | solution.py:109
  345.3 1.4 convolution_bitcast_fusion.3
  346.7 256.0 %psum.22 = f32[16,16]{0,1:T(8,128)S(1)} all-reduce(f32[16,16]{0,1:T(8,128)S(1)} %convolution_bitcast_fusion.3), channel_id=1, replica_groups=mesh['space'=128,'basis'=4] {'space'}, use_global_device_ids=true, to_apply=%region_2.3 | all-reduce | flops 256 | bytes 2048 | tf_op jit(solution)/shard_map/psum | solution.py:74
  602.7 1.1 convolution_bitcast_fusion
  603.9 1.1 copy.128
  605.1 0.7 copy.86
  605.8 24.7 %reduce-scatter.11.cloned.1.call-done = f32[8,6144]{1,0:T(8,128)} async-done(((f32[32,6144]{1,0:T(8,128)}), f32[8,6144]{1,0:T(8,128)}) %reduce-scatter.11.cloned.1.call-update) | async-done | bytes 196624
  630.5 1.0 copy.110
  631.5 0.3 convolution_bitcast_fusion.6
  631.8 105.2 %psum.23 = f32[16,16]{0,1:T(8,128)S(1)} all-reduce(f32[16,16]{0,1:T(8,128)S(1)} %convolution_bitcast_fusion.6), channel_id=1, replica_groups=mesh['space'=128,'basis'=4] {'space','basis'}, use_global_device_ids=true, to_apply=%region_4.5 | all-reduce | flops 256 | bytes 2048 | tf_op jit(solution)/shard_map/psum | solution.py:89
  737.1 1.5 cholesky.17
  738.6 0.6 compare_reduce_fusion
  739.2 0.6 fusion.15
  739.9 0.7 copy.87
  740.6 1.2 custom-call.7
  741.8 0.2 convolution_bitcast_fusion.5
  742.0 0.3 convolution_bitcast_fusion.2
  742.3 0.7 copy.85
  (43 shorter events, 0.7 us)
Async XLA Ops:
  7.2 38.7 %copy-start = (f32[16,3,1,32,128]{4,3,2,1,0:T(8,128)S(1)}, f32[16,3,1,32,128]{4,3,2,1,0:T(8,128)}, u32[]{:S(2)}) copy-start(f32[16,3,1,32,128]{4,3,2,1,0:T(8,128)} %param.13) | copy-start | bytes 2359300
  7.2 326.0 %reduce-scatter.9.cloned.1.call-start = ((), (), s32[]{:S(2)}) async-start(), calls=%async_computation.2 | async-start | bytes 983040
  7.2 16.3 %copy-start.4 = (s32[1,8,128]{2,1,0:T(8,128)S(1)}, s32[1,8,128]{2,1,0:T(8,128)}, u32[]{:S(2)}) copy-start(s32[1,8,128]{2,1,0:T(8,128)} %param.14) | copy-start | bytes 12292
  7.2 16.3 %copy-start.5 = (f32[8,3]{0,1:T(4,128)S(1)}, f32[8,3]{0,1:T(4,128)}, u32[]{:S(2)}) copy-start(f32[8,3]{0,1:T(4,128)} %param.16) | copy-start | bytes 292
  7.2 16.3 %copy-start.6 = (f32[8,3]{0,1:T(4,128)S(1)}, f32[8,3]{0,1:T(4,128)}, u32[]{:S(2)}) copy-start(f32[8,3]{0,1:T(4,128)} %param.18) | copy-start | bytes 292
  8.3 18.2 %collective-permute-start.1 = (f32[16,3,1,8,128]{4,0,3,1,2:T(8,128)S(1)}, f32[16,3,1,8,128]{4,0,3,1,2:T(8,128)S(1)}, u32[]{:S(2)}, u32[]{:S(2)}) collective-permute-start(f32[16,3,1,8,128]{4,0,3,1,2:T(8,128)S(1)} %copy.71), channel_id=1, source_target_pairs={{4,0},{8,4},{12,8},{16,12},{20,16},{24,20},{28,24},{32,28},{36,32}... | collective-permute-start | bytes 589832 | tf_op jit(solution)/shard_map/ppermute | solution.py:19
  17.1 8.5 %collective-permute-start = (f32[16,3,1,8,128]{4,0,3,1,2:T(8,128)S(1)}, f32[16,3,1,8,128]{4,0,3,1,2:T(8,128)S(1)}, u32[]{:S(2)}, u32[]{:S(2)}) collective-permute-start(f32[16,3,1,8,128]{4,0,3,1,2:T(8,128)S(1)} %copy.71), channel_id=1, source_target_pairs={{0,4},{4,8},{8,12},{12,16},{16,20},{20,24},{24,28},{28,32},{32,36}... | collective-permute-start | bytes 589832 | tf_op jit(solution)/shard_map/ppermute | solution.py:17
  19.0 4.6 copy-start.3
  19.0 4.6 copy-start.2
  25.5 0.9 copy-start.1
  26.6 5.3 collective-permute-start.3
  27.9 5.4 collective-permute-start.2
  306.3 324.3 %reduce-scatter.11.cloned.1.call-start = ((), (), s32[]{:S(2)}) async-start(), calls=%async_computation.3 | async-start | bytes 983040
Sparse Core Ops, SparseCore 0:
  306.4 26.7 reduce-scatter.8
  605.2 25.2 reduce-scatter.10
where the time goes:
time: 750 us
  blocking collectives  641 us (85%)
  waiting for transfers between devices  53 us (7%)
  between operations  16.4 us (2%)
  starting transfers between devices  16.1 us (2%)
  local copies, waits for them, and re-layouts  12.2 us (2%)
    psum x2, blocking collectives, group_sum(): return lax.psum(partial_value, 'space')  513 us
    psum x1, blocking collectives, finish(): gram_matrix = lax.psum(gram_partial, ('space', 'basis')) / row_count  105 us
    unnamed x4, waiting for transfers between devices  51.6 us
    all_gather x2, blocking collectives, shards(): lax.all_gather(fine_block, 'basis', axis=3, tiled=True)  23 us
  transfers between devices with their start and end apart: 6, of which 3 were waited for; matrix products, arithmetic and copies ran while one was open for 1% of the time, Pallas kernels for 0%

commit v1 on v0

--- a/solution.py
+++ b/solution.py
@@ -86,7 +86,7 @@
 
 def finish(fine_block, row_count):
     gram_partial = jnp.einsum("ncxyz,mcxyz->nm", fine_block, fine_block, precision=exact_precision)
-    gram_matrix = lax.psum(gram_partial, ("space", "basis")) / row_count
+    gram_matrix = jnp.sum(lax.all_gather(gram_partial, ("space", "basis")), axis=0) / row_count
     return scaled_block(fine_block, gram_matrix)
 
 

time: 750 us -> 801 us (1.068)
  blocking collectives: 641 us -> 681 us
    all_gather x0 -> x1, blocking collectives: none -> 145 us  [finish(): lax.all_gather(gram_partial, ('space', 'basis'))]
    psum x1 -> x0, blocking collectives: 105 us -> none  [finish(): gram_matrix = lax.psum(gram_partial, ('space', 'basis')) / row_count]
where the time goes in v1:
time: 801 us; the launch traced here: 795 us
  blocking collectives  681 us (85%)
  waiting for transfers between devices  53 us (7%)
  between operations  16.3 us (2%)
  starting transfers between devices  16.1 us (2%)
  local copies, waits for them, and re-layouts  12.2 us (2%)
  other arithmetic  10.3 us (1%)
    psum x2, blocking collectives, group_sum(): return lax.psum(partial_value, 'space')  513 us
    all_gather x1, blocking collectives, finish(): lax.all_gather(gram_partial, ('space', 'basis'))  145 us
    unnamed x4, waiting for transfers between devices  51.6 us
    all_gather x2, blocking collectives, shards(): lax.all_gather(fine_block, 'basis', axis=3, tiled=True)  23 us
  transfers between devices with their start and end apart: 6, of which 3 were waited for; matrix products, arithmetic and copies ran while one was open for 1% of the time, Pallas kernels for 0%

profile of v1, /device:TPU:1, one launch (start us, length us, event | category | flops | bytes accessed | tf_op | source)
XLA Modules:
  0.0 795.0 jit_solution(9616697629399981944)
XLA Ops:
  7.2 1.0 copy.69
  8.3 8.8 %collective-permute-start.1 = (f32[16,3,1,8,128]{4,0,3,1,2:T(8,128)S(1)}, f32[16,3,1,8,128]{4,0,3,1,2:T(8,128)S(1)}, u32[]{:S(2)}, u32[]{:S(2)}) collective-permute-start(f32[16,3,1,8,128]{4,0,3,1,2:T(8,128)S(1)} %copy.69), channel_id=1, source_target_pairs={{4,0},{8,4},{12,8},{16,12},{20,16},{24,20},{28,24},{32,28},{36,32}... | collective-permute-start | bytes 589832 | tf_op jit(solution)/shard_map/ppermute | solution.py:19
  17.1 1.9 collective-permute-start
  19.6 1.3 dynamic-slice.13
  20.9 1.3 dynamic-slice.12
  23.5 0.7 convert_bitcast_fusion.7
  24.2 0.7 multiply_subtract_fusion.1
  24.9 0.8 multiply_subtract_fusion
  25.9 0.1 copy.92
  26.0 0.1 copy.99
  26.1 0.1 copy.98
  26.2 0.1 copy.97
  26.3 0.1 copy.96
  26.8 0.6 multiply_add_fusion
  27.4 0.1 fusion.22
  27.6 1.0 constant_dynamic-update-slice_fusion.1
  28.6 1.3 collective-permute-start.3
  29.9 4.0 collective-permute-start.2
  33.9 1.4 collective-permute-done.2
  35.3 0.2 add_add_fusion.2
  35.5 0.2 add_add_fusion.1
  35.7 0.2 add_add_fusion
  36.0 11.9 %all_gather.12 = f32[16,3,1,32,128]{4,0,3,1,2:T(8,128)S(1)} all-gather(f32[16,3,1,8,128]{4,0,3,1,2:T(8,128)S(1)} %pad_maximum_fusion), channel_id=1, replica_groups=mesh['space'=128,'basis'=4] {'basis'}, dimensions={3}, use_global_device_ids=true | all-gather | bytes 983040 | tf_op jit(solution)/shard_map/all_gather | solution.py:109
  47.9 1.4 convolution_bitcast_fusion.4
  49.3 256.7 %psum.14 = f32[16,16]{0,1:T(8,128)S(1)} all-reduce(f32[16,16]{0,1:T(8,128)S(1)} %convolution_bitcast_fusion.4), channel_id=1, replica_groups=mesh['space'=128,'basis'=4] {'space'}, use_global_device_ids=true, to_apply=%region_0.1 | all-reduce | flops 256 | bytes 2048 | tf_op jit(solution)/shard_map/psum | solution.py:74
  305.9 1.1 convolution_bitcast_fusion.1
  307.2 1.1 copy.126
  308.4 26.9 %reduce-scatter.9.cloned.1.call-done = f32[8,6144]{1,0:T(8,128)} async-done(((f32[32,6144]{1,0:T(8,128)}), f32[8,6144]{1,0:T(8,128)}) %reduce-scatter.9.cloned.1.call-update) | async-done | bytes 196624
  335.2 1.0 copy.105
  336.2 11.1 %all_gather.13 = f32[16,3,1,32,128]{4,0,3,1,2:T(8,128)S(1)} all-gather(f32[16,3,1,8,128]{4,0,3,1,2:T(8,128)S(1)} %copy_subtract_fusion.1), channel_id=1, replica_groups=mesh['space'=128,'basis'=4] {'basis'}, dimensions={3}, use_global_device_ids=true | all-gather | bytes 983040 | tf_op jit(solution)/shard_map/all_gather | solution.py:109
  347.4 1.4 convolution_bitcast_fusion.3
  348.8 256.0 %psum.15 = f32[16,16]{0,1:T(8,128)S(1)} all-reduce(f32[16,16]{0,1:T(8,128)S(1)} %convolution_bitcast_fusion.3), channel_id=1, replica_groups=mesh['space'=128,'basis'=4] {'space'}, use_global_device_ids=true, to_apply=%region_2.3 | all-reduce | flops 256 | bytes 2048 | tf_op jit(solution)/shard_map/psum | solution.py:74
  604.8 1.1 convolution_bitcast_fusion
  606.0 1.1 copy.125
  607.2 0.7 copy.84
  607.8 24.7 %reduce-scatter.11.cloned.1.call-done = f32[8,6144]{1,0:T(8,128)} async-done(((f32[32,6144]{1,0:T(8,128)}), f32[8,6144]{1,0:T(8,128)}) %reduce-scatter.11.cloned.1.call-update) | async-done | bytes 196624
  632.5 1.0 copy.107
  633.5 0.3 convolution_bitcast_fusion.6
  633.8 145.4 %all-gather = f32[8192,16]{1,0:T(8,128)} all-gather(f32[16,16]{1,0:T(8,128)S(1)} %convolution_bitcast_fusion.6), channel_id=2, replica_groups=mesh['space'=128,'basis'=4] {'space','basis'}, dimensions={0}, use_global_device_ids=true | all-gather | bytes 525312 | tf_op jit(solution)/shard_map/all_gather | solution.py:89
  779.3 2.7 reduce_sum.9
  782.2 1.5 cholesky.17
  783.6 0.6 compare_reduce_fusion
  784.3 0.6 fusion.15
  785.0 0.7 copy.85
  785.6 1.2 custom-call.7
  786.9 0.2 convolution_bitcast_fusion.5
  787.0 0.3 convolution_bitcast_fusion.2
  787.4 0.7 copy.83
  (33 shorter events, 1.1 us)
Async XLA Ops:
  7.2 40.7 %copy-start = (f32[16,3,1,32,128]{4,3,2,1,0:T(8,128)S(1)}, f32[16,3,1,32,128]{4,3,2,1,0:T(8,128)}, u32[]{:S(2)}) copy-start(f32[16,3,1,32,128]{4,3,2,1,0:T(8,128)} %param.13) | copy-start | bytes 2359300
  7.2 328.1 %reduce-scatter.9.cloned.1.call-start = ((), (), s32[]{:S(2)}) async-start(), calls=%async_computation.2 | async-start | bytes 983040
  8.3 20.3 %collective-permute-start.1 = (f32[16,3,1,8,128]{4,0,3,1,2:T(8,128)S(1)}, f32[16,3,1,8,128]{4,0,3,1,2:T(8,128)S(1)}, u32[]{:S(2)}, u32[]{:S(2)}) collective-permute-start(f32[16,3,1,8,128]{4,0,3,1,2:T(8,128)S(1)} %copy.69), channel_id=1, source_target_pairs={{4,0},{8,4},{12,8},{16,12},{20,16},{24,20},{28,24},{32,28},{36,32}... | collective-permute-start | bytes 589832 | tf_op jit(solution)/shard_map/ppermute | solution.py:19
  17.1 10.5 %collective-permute-start = (f32[16,3,1,8,128]{4,0,3,1,2:T(8,128)S(1)}, f32[16,3,1,8,128]{4,0,3,1,2:T(8,128)S(1)}, u32[]{:S(2)}, u32[]{:S(2)}) collective-permute-start(f32[16,3,1,8,128]{4,0,3,1,2:T(8,128)S(1)} %copy.69), channel_id=1, source_target_pairs={{0,4},{4,8},{8,12},{12,16},{16,20},{20,24},{24,28},{28,32},{32,36}... | collective-permute-start | bytes 589832 | tf_op jit(solution)/shard_map/ppermute | solution.py:17
  28.6 5.3 collective-permute-start.3
  29.9 5.4 collective-permute-start.2
  308.3 324.2 %reduce-scatter.11.cloned.1.call-start = ((), (), s32[]{:S(2)}) async-start(), calls=%async_computation.3 | async-start | bytes 983040
Sparse Core Ops, SparseCore 0:
  308.4 26.7 reduce-scatter.8
  607.3 25.2 reduce-scatter.10
